TPU v7x, 32 devices: a whole 2x2x4 slice. The times are simulated.
32 devices in a mesh: row: 16 (over z, y, core), col: 2 (over x).
Axes of the slice: x: 2, y: 2, z: 4, core: 2. Of those that a mesh axis runs over, the one named last changes fastest.
Arguments:
- left: float32 [128, 8192], P('col', 'row'), may hold values from -12 to 12
- right: float32 [128, 8192], P('row', 'col'), may hold values from -12 to 12
- w_out: float32 [1024, 128], replicated, may hold values from -0.1875 to 0.1875
- b_out: float32 [128], replicated, may hold values from -3 to 3
- pair_grad: float32 [256, 256, 128], P('row', 'col'), may hold values from -6 to 6
Outputs:
- pair_out: float32 [256, 256, 128], P('row', 'col')
- grad_left: float32 [128, 8192], P('col', 'row')
- grad_right: float32 [128, 8192], P('row', 'col')
- grad_weight: float32 [1024, 128], replicated
- grad_bias: float32 [128], replicated
All inputs are finite; a program needn't handle non-finite values.
Results may differ from a plain program's by a relative error of at most 0.0001.
Values sent between devices are 32-bit elements; how exact they have to be, the bound alone decides.
A program may use at most 128 MiB of HBM per device.

v0:
```python
import jax
import jax.numpy as jnp
from jax import lax
from jax.sharding import PartitionSpec as P

C = 32
Z = 128
S = 128


def body(left, right, w_out, b_out, pair_grad):
    highest = lax.Precision.HIGHEST
    tile_rows = left.shape[1] // C
    tile_cols = right.shape[1] // C
    residues = tile_rows * lax.axis_size("row")
    weight_cube = w_out.reshape(C, C, Z)
    contract_rows = (((0,), (0,)), ((), ()))
    contract_cols = (((1,), (1,)), ((), ()))
    left_all = lax.all_gather(left, "col", axis=0, tiled=True)
    right_all = lax.all_gather(right, "row", axis=0, tiled=True)
    outer = (
        lax.dot_general(
            left_all,
            right_all,
            contract_rows,
            precision=highest,
            preferred_element_type=jnp.float32,
        )
        / S
    )
    outer_split = outer.reshape(tile_rows, C, tile_cols, C)
    pair_out = jnp.einsum("icje,cez->ijz", outer_split, weight_cube, precision=highest) + b_out
    grad_outer = jnp.einsum("ijz,cez->icje", pair_grad, weight_cube, precision=highest)
    grad_outer = grad_outer.reshape(tile_rows * C, tile_cols * C)
    grad_left = lax.psum_scatter(
        lax.dot_general(
            right_all,
            grad_outer,
            contract_cols,
            precision=highest,
            preferred_element_type=jnp.float32,
        )
        / S,
        "col",
        scatter_dimension=0,
        tiled=True,
    )
    grad_right = lax.psum_scatter(
        jnp.dot(left_all, grad_outer, precision=highest) / S, "row", scatter_dimension=0, tiled=True
    )
    weight_term = jnp.einsum("icje,ijz->cez", outer_split, pair_grad, precision=highest).reshape(
        C * C, Z
    )
    bias_term = jnp.sum(pair_grad, axis=(0, 1))
    grad_weight, grad_bias = lax.psum((weight_term, bias_term), ("row", "col"))
    return (pair_out, grad_left, grad_right, grad_weight / residues, grad_bias / residues)


def solution(mesh):
    placed = (P("col", "row"), P("row", "col"), P(), P(), P("row", "col", None))
    return jax.shard_map(
        body,
        mesh=mesh,
        in_specs=placed,
        out_specs=(P("row", "col", None), P("col", "row"), P("row", "col"), P(), P()),
        check_vma=False,
    )
```

profile of v0, /device:TPU:0, one launch (start us, length us, event | category | flops | bytes accessed | tf_op | source)
XLA Modules:
  0.0 346.1 jit_solution(6680245117973398860)
XLA Ops:
  7.2 0.0 copy-start
  7.2 0.0 all-gather.2.cloned.1.call-start
  7.2 0.7 all-gather.2.cloned.1.call-update
  7.9 0.0 all-reduce.2.cloned.1.call-start
  8.0 0.3 copy-done
  8.2 9.8 %convolution_bitcast_fusion = f32[16,32,128,32]{2,3,0,1:T(8,128)} fusion(f32[32,32,128,1]{2,1,3,0:T(8,128)S(1)} %bitcast.40, f32[16,128,128]{2,1,0:T(8,128)} %param.9), kind=kOutput, calls=%fused_computation.3 | convolution fusion | flops 3221225472 | bytes 9961472 | tf_op jit(solution)/shard_map/ijz,cez->icje/dot_general | solution.py:33
  18.0 19.7 %copy.25 = f32[16,32,128,32]{3,2,1,0:T(8,128)} copy(f32[16,32,128,32]{2,3,0,1:T(8,128)} %convolution_bitcast_fusion) | data formatting | bytes 16777216 | tf_op jit(solution)/shard_map/ijz,cez->icje/transpose | solution.py:33
  37.7 0.0 copy-start.2
  37.8 24.6 %reshape.24 = f32[512,4096]{1,0:T(8,128)} reshape(f32[16,32,128,32]{3,2,1,0:T(8,128)} %copy.25) | data formatting | bytes 16777216 | tf_op jit(solution)/shard_map/reshape | solution.py:34
  62.4 0.0 copy-done.2
  62.4 7.2 %all_gather.6 = f32[128,512]{1,0:T(8,128)S(1)} all-gather(f32[64,512]{1,0:T(8,128)S(1)} %copy-done.2), channel_id=1, replica_groups=mesh['row'=16,'col'=2] {'col'}, dimensions={0}, use_global_device_ids=true | all-gather | bytes 393216 | tf_op jit(solution)/shard_map/all_gather | solution.py:19
  69.6 0.0 all-gather.2.cloned.1.call-done
  69.6 10.1 %convolution_multiply_fusion = f32[512,4096]{1,0:T(8,128)} fusion(f32[128,512]{1,0:T(8,128)S(1)} %all_gather.6, f32[128,4096]{1,0:T(8,128)} %all-gather.2.cloned.1.call-done), kind=kOutput, calls=%fused_computation | convolution fusion | flops 3223322624 | bytes 10747904 | tf_op jit(solution)/shard_map/dot_general | solution.py:22
  79.7 20.1 %reshape.22 = f32[16,32,128,32]{3,2,1,0:T(8,128)} reshape(f32[512,4096]{1,0:T(8,128)} %convolution_multiply_fusion) | data formatting | bytes 16777216 | tf_op jit(solution)/shard_map/reshape | solution.py:31
  99.9 0.0 copy-start.1
  99.9 21.8 %copy.33 = f32[32,32,16,128]{3,1,0,2:T(8,128)} copy(f32[32,32,16,128]{1,3,0,2:T(8,128)} %bitcast.41) | data formatting | bytes 16777216 | tf_op jit(solution)/shard_map/icje,ijz->cez/dot_general | solution.py:51
  121.6 0.0 copy-done.1
  121.7 9.7 %convolution_bitcast_fusion.2 = f32[1024,128]{1,0:T(8,128)} fusion(f32[1024,16,128]{2,0,1:T(8,128)} %bitcast.42, f32[16,128,128]{2,1,0:T(8,128)S(1)} %copy-done.1), kind=kOutput, calls=%fused_computation.6 | convolution fusion | flops 3221225472 | bytes 9961472 | tf_op jit(solution)/shard_map/icje,ijz->cez/dot_general | solution.py:51
  131.4 0.0 all-reduce.2.cloned.1.call-update
  131.4 0.3 reduce-scatter.9.cloned.1.call-start
  131.7 15.6 %fusion = f32[128,4096]{0,1:T(8,128)S(1)} fusion(f32[512,4096]{1,0:T(8,128)} %reshape.24, f32[128,512]{1,0:T(8,128)S(1)} %all_gather.6), kind=kOutput, calls=%fused_computation.2 | convolution fusion | flops 3221749760 | bytes 10747904 | tf_op jit(solution)/shard_map/dot_general | solution.py:49
  147.3 1.8 copy.36
  149.1 0.0 reduce-scatter.9.cloned.1.call-update
  149.2 0.0 copy-start.3
  149.2 0.0 reduce-scatter.7.cloned.1.call-start
  149.2 1.5 reduce_sum.9
  150.7 41.2 %psum.15 = f32[128]{0:T(128)S(1)} all-reduce(f32[128]{0:T(128)S(1)} %reduce_sum.9), channel_id=1, replica_groups=mesh['row'=16,'col'=2] {'row','col'}, use_global_device_ids=true, to_apply=%region_4.0 | all-reduce | flops 128 | bytes 1024 | tf_op jit(solution)/shard_map/psum | solution.py:55
  191.9 0.5 broadcast_multiply_fusion.1
  192.4 9.4 %fusion.2 = f32[128,512]{0,1:T(8,128)S(1)} fusion(f32[512,4096]{1,0:T(8,128)} %reshape.24, f32[128,4096]{1,0:T(8,128)} %all-gather.2.cloned.1.call-done), kind=kOutput, calls=%fused_computation.8 | convolution fusion | flops 3221291008 | bytes 10747904 | tf_op jit(solution)/shard_map/dot_general | solution.py:36
  201.8 0.8 copy.34
  202.6 0.0 reduce-scatter.7.cloned.1.call-update
  202.7 0.0 copy-done.3
  202.7 31.3 %fusion.1 = f32[16,128,128]{2,1,0:T(8,128)} fusion(f32[16,32,128,32]{3,2,1,0:T(8,128)} %reshape.22, f32[32,32,128,1]{2,1,0,3:T(8,128)S(1)} %bitcast.39, f32[128]{0:T(128)S(1)} %copy-done.3), kind=kOutput, calls=%fused_computation.5 | convolution fusion | flops 3221487616 | bytes 9961984 | tf_op jit(solution)/shard_map/icje,cez->ijz/dot_general | solution.py:32
  234.0 26.9 %all-reduce.2.cloned.1.call-done = f32[1024,128]{1,0:T(8,128)} async-done(((f32[1024,128]{1,0:T(8,128)}), f32[1024,128]{1,0:T(8,128)}) %all-reduce.2.cloned.1.call-update) | async-done | bytes 524304 | tf_op jit(solution)/shard_map/psum | solution.py:55
  260.9 1.9 broadcast_multiply_fusion
  262.8 63.5 %reduce-scatter.9.cloned.1.call-done = f32[8,4096]{1,0:T(8,128)} async-done(((f32[128,4096]{1,0:T(8,128)}), f32[8,4096]{1,0:T(8,128)}) %reduce-scatter.9.cloned.1.call-update) | async-done | bytes 131088
  326.3 13.3 %reduce-scatter.7.cloned.1.call-done = f32[64,512]{1,0:T(8,128)} async-done(((f32[128,512]{1,0:T(8,128)}), f32[64,512]{1,0:T(8,128)}) %reduce-scatter.7.cloned.1.call-update) | async-done | bytes 131088
Async XLA Ops:
  7.2 1.0 copy-start
  7.2 62.4 %all-gather.2.cloned.1.call-start = ((), (), s32[]{:S(2)}) async-start(), calls=%async_computation.2 | async-start | bytes 2228224 | tf_op jit(solution)/shard_map/all_gather | solution.py:20
  7.9 253.0 %all-reduce.2.cloned.1.call-start = ((), (), s32[]{:S(2)}) async-start(), calls=%async_computation.3 | async-start | bytes 1048576 | tf_op jit(solution)/shard_map/psum | solution.py:55
  37.7 24.6 %copy-start.2 = (f32[64,512]{1,0:T(8,128)S(1)}, f32[64,512]{1,0:T(8,128)}, u32[]{:S(2)}) copy-start(f32[64,512]{1,0:T(8,128)} %param.5) | copy-start | bytes 393220
  99.9 21.8 %copy-start.1 = (f32[16,128,128]{2,1,0:T(8,128)S(1)}, f32[16,128,128]{2,1,0:T(8,128)}, u32[]{:S(2)}) copy-start(f32[16,128,128]{2,1,0:T(8,128)} %param.9) | copy-start | bytes 3145732
  131.4 194.8 %reduce-scatter.9.cloned.1.call-start = ((), (), s32[]{:S(2)}) async-start(), calls=%async_computation.5 | async-start | bytes 2228224
  149.2 53.5 %copy-start.3 = (f32[128]{0:T(128)S(1)}, f32[128]{0:T(128)}, u32[]{:S(2)}) copy-start(f32[128]{0:T(128)} %param.8) | copy-start | bytes 1540
  149.2 190.4 %reduce-scatter.7.cloned.1.call-start = ((), (), s32[]{:S(2)}) async-start(), calls=%async_computation.4 | async-start | bytes 393216
Sparse Core Ops, SparseCore 0:
  10.2 44.1 all-gather.1
  131.5 129.3 all-reduce.1
  265.7 60.5 reduce-scatter.8
  328.9 10.6 reduce-scatter.6
where the time goes:
time: 348 us; the launch traced here: 346 us
  waiting for transfers between devices  104 us (30%)
  local copies, waits for them, and re-layouts  89.2 us (26%)
  matrix products  86 us (25%)
  blocking collectives  48.4 us (14%)
  between operations  13.8 us (4%)
  other arithmetic  3.9 us (1%)
    unnamed x6, waiting for transfers between devices  77.5 us
    psum x1, blocking collectives, body(): grad_weight, grad_bias = lax.psum((weight_term, bias_term), ('row', 'col'))  41.2 us
    dot_general x1, matrix products, body(): jnp.einsum('icje,cez->ijz', outer_split, weight_cube, precision=highest)  31.3 us
    psum x1, waiting for transfers between devices, body(): grad_weight, grad_bias = lax.psum((weight_term, bias_term), ('row', 'col'))  26.9 us
    reshape x1, local copies, waits for them, and re-layouts, body(): grad_outer = grad_outer.reshape(tile_rows * C, tile_cols * C)  24.6 us
    dot_general x1, local copies, waits for them, and re-layouts, body(): jnp.einsum('icje,ijz->cez', outer_split, pair_grad, precision=highest)  21.8 us
    reshape x1, local copies, waits for them, and re-layouts, body(): outer_split = outer.reshape(tile_rows, C, tile_cols, C)  20.1 us
    transpose x1, local copies, waits for them, and re-layouts, body(): jnp.einsum('ijz,cez->icje', pair_grad, weight_cube, precision=highest)  19.7 us
  transfers between devices with their start and end apart: 4, of which 3 were waited for; matrix products, arithmetic and copies ran while one was open for 34% of the time, Pallas kernels for 0%

commit v1 on v0

v1 whole, which is shorter than its diff:
```python
import functools

import jax
import jax.numpy as jnp
from jax import lax
from jax.experimental import pallas as pl
from jax.experimental.pallas import tpu as pltpu
from jax.sharding import PartitionSpec as P

C = 32
Z = 128
S = 128
LANES = 128
BF = jnp.bfloat16
F32 = jnp.float32
NN = (((1,), (0,)), ((), ()))
NT = (((1,), (1,)), ((), ()))


def split(x):
    high = x.astype(BF)
    return high, (x - high.astype(F32)).astype(BF)


def mm(a, b, dims):
    return lax.dot_general(a, b, dims, preferred_element_type=F32)


def split_grad(pg, pgh, pgl, gb):
    rows = pg.shape[0]
    step = min(rows, 512)

    def one(k, total):
        at = pl.ds(pl.multiple_of(k * step, step), step)
        x = pg[at, :]
        high, low = split(x)
        pgh[at, :] = high
        pgl[at, :] = low
        return total + jnp.sum(x.reshape(step // 8, 8, x.shape[1]), axis=0)

    total = lax.fori_loop(0, rows // step, one, jnp.zeros((8, pg.shape[1]), F32))
    gb[...] = jnp.sum(total, axis=0, keepdims=True)


def make_grad_outer(pgh, pgl, w, gh, gl, tj):
    wh, wl = split(w[...])
    both = jnp.concatenate([wh, wl], axis=1)
    group = 2

    def one(k, carry):
        at = pl.ds(pl.multiple_of(k * group * tj, group * tj), group * tj)
        ph, low = pgh[at, :], pgl[at, :]
        g = mm(both, jnp.concatenate([ph, ph], axis=1), NT) + mm(wh, low, NT)
        high, low = split(g)
        for i in range(group):
            rows = pl.ds(pl.multiple_of(k * group * C + i * C, C), C)
            for e in range(C):
                gh[rows, e * tj : (e + 1) * tj] = high[e * C : (e + 1) * C, i * tj : (i + 1) * tj]
                gl[rows, e * tj : (e + 1) * tj] = low[e * C : (e + 1) * C, i * tj : (i + 1) * tj]
        return carry

    lax.fori_loop(0, pgh.shape[0] // (group * tj), one, 0)


def make_grad_right(a, gh, gl, put, width):
    ah, al = split(a[...])
    both = jnp.concatenate([ah, al], axis=0)

    def one(k, carry):
        cols = pl.ds(pl.multiple_of(k * width, width), width)
        high, low = gh[:, cols], gl[:, cols]
        r = mm(both, high, NN)
        r = r[:S] + r[S:] + mm(ah, low, NN)
        put(cols, r * (1.0 / S))
        return carry

    lax.fori_loop(0, gh.shape[1] // width, one, 0)


def make_outer(a, bh, bl, oh, ol, tj):
    ath, atl = split(a[...].T * (1.0 / S))
    both = jnp.concatenate([ath, atl], axis=1)
    ti = a.shape[1] // C
    group = 4
    width = group * tj

    def one(k, carry):
        cols = pl.ds(pl.multiple_of(k * width, width), width)
        high, low = bh[:, cols], bl[:, cols]
        o = mm(both, jnp.concatenate([high, high], axis=0), NN) + mm(ath, low, NN)
        high, low = split(o)
        for e in range(group):
            rows = pl.ds(pl.multiple_of(k * group * C + e * C, C), C)
            for i in range(ti):
                oh[rows, i * tj : (i + 1) * tj] = high[i * C : (i + 1) * C, e * tj : (e + 1) * tj]
                ol[rows, i * tj : (i + 1) * tj] = low[i * C : (i + 1) * C, e * tj : (e + 1) * tj]
        return carry

    lax.fori_loop(0, bh.shape[1] // width, one, 0)


def make_grad_weight(oh, ol, pgh, pgl, gw, scale):
    step = 256

    def one(k, carry):
        rows = pl.ds(pl.multiple_of(k * step, step), step)
        ph = pgh[...]
        r = mm(oh[rows, :], jnp.concatenate([ph, pgl[...]], axis=1), NN)
        gw[rows, :] = (r[:, :Z] + r[:, Z:] + mm(ol[rows, :], ph, NN)) * scale
        return carry

    lax.fori_loop(0, oh.shape[0] // step, one, 0)


def make_pair_out(oh, ol, w, bias, out, width):
    wh, wl = split(w[...].T)
    both = jnp.concatenate([wh, wl], axis=0)

    def one(k, carry):
        cols = pl.ds(pl.multiple_of(k * width, width), width)
        r = mm(both, oh[:, cols], NN)
        r = r[:Z] + r[Z:] + mm(wh, ol[:, cols], NN)
        out[cols, :] = r.T + bias[...]
        return carry

    lax.fori_loop(0, oh.shape[1] // width, one, 0)


def make_grad_left(bh, bl, gh, gl, put, step):
    both = jnp.concatenate([bh[...], bl[...]], axis=0)
    for k in range(gh.shape[0] // step):
        rows = slice(k * step, (k + 1) * step)
        r = mm(both, gh[rows, :], NT)
        r = r[:S] + r[S:] + mm(bh[...], gl[rows, :], NT)
        put(rows, r * (1.0 / S))


def first_kernel(tj, a, pg, w, gr, gh, gl, pgh, pgl, gb):
    split_grad(pg, pgh, pgl, gb)
    make_grad_outer(pgh, pgl, w, gh, gl, tj)

    def put(cols, r):
        gr[:, cols] = r

    make_grad_right(a, gh, gl, put, 4 * tj)


def second_kernel(tj, scale, a, b, w, bias, gh, gl, pgh, pgl, out, left, gw, bh, bl, oh, ol):
    high, low = split(b[...])
    bh[...] = high
    bl[...] = low
    make_outer(a, bh, bl, oh, ol, tj)
    make_grad_weight(oh, ol, pgh, pgl, gw, scale)

    def put(cols, r):
        left[:, cols] = r

    make_grad_left(bh, bl, gh, gl, put, 256)
    make_pair_out(oh, ol, w, bias, out, 2 * tj)


def fast(left, right, w_out, b_out, pair_grad):
    ti = left.shape[1] // C
    tj = right.shape[1] // C
    pairs = ti * tj
    residues = ti * lax.axis_size("row")
    scale = 1.0 / residues
    vmem = pl.BlockSpec(memory_space=pltpu.VMEM)
    params = pltpu.CompilerParams(vmem_limit_bytes=56 * 1024 * 1024)
    w = w_out.reshape(C, C, Z).transpose(1, 0, 2).reshape(C * C, Z)
    pg = pair_grad.reshape(pairs, Z)
    mine = right.reshape(-1, tj, C).transpose(0, 2, 1).reshape(right.shape)
    a = lax.all_gather(left, "col", axis=0, tiled=True)
    b = lax.all_gather(mine, "row", axis=0, tiled=True)
    flops = 2 * pairs * C * C * Z * 3
    shape = jax.ShapeDtypeStruct
    gr, gh, gl, pgh, pgl, gb = pl.pallas_call(
        functools.partial(first_kernel, tj),
        out_shape=[
            shape((S, C * tj), F32),
            shape((ti * C, C * tj), BF),
            shape((ti * C, C * tj), BF),
            shape((pairs, Z), BF),
            shape((pairs, Z), BF),
            shape((1, Z), F32),
        ],
        in_specs=[vmem] * 3,
        out_specs=[vmem] * 6,
        compiler_params=params,
        cost_estimate=pl.CostEstimate(flops=2 * flops, bytes_accessed=1 << 24, transcendentals=0),
        name="grads_of_outer",
    )(a, pg, w)
    grad_right = lax.psum_scatter(gr, "row", scatter_dimension=0, tiled=True)
    out, part, gw = pl.pallas_call(
        functools.partial(second_kernel, tj, scale),
        out_shape=[
            shape((pairs, Z), F32),
            shape((S, ti * C), F32),
            shape((C * C, Z), F32),
        ],
        in_specs=[vmem] * 8,
        out_specs=[vmem] * 3,
        scratch_shapes=[
            pltpu.VMEM((S, C * tj), BF),
            pltpu.VMEM((S, C * tj), BF),
            pltpu.VMEM((C * C, pairs), BF),
            pltpu.VMEM((C * C, pairs), BF),
        ],
        compiler_params=params,
        cost_estimate=pl.CostEstimate(flops=4 * flops, bytes_accessed=1 << 24, transcendentals=0),
        name="outer_and_rest",
    )(a, b, w, b_out.reshape(1, Z), gh, gl, pgh, pgl)
    grad_left = lax.psum_scatter(part, "col", scatter_dimension=0, tiled=True)
    gb8 = jnp.broadcast_to(gb * (scale / 8), (8, Z))
    total = lax.psum(jnp.concatenate([gw, gb8], axis=0), ("row", "col"))
    grad_weight = total[: C * C].reshape(C, C, Z).transpose(1, 0, 2).reshape(C * C, Z)
    grad_bias = jnp.sum(total[C * C :], axis=0)
    grad_right = grad_right.reshape(-1, C, tj).transpose(0, 2, 1).reshape(right.shape)
    return (out.reshape(pair_grad.shape), grad_left, grad_right, grad_weight, grad_bias)


def plain(left, right, w_out, b_out, pair_grad):
    high = lax.Precision.HIGHEST
    ti = left.shape[1] // C
    tj = right.shape[1] // C
    residues = ti * lax.axis_size("row")
    cube = w_out.reshape(C, C, Z)
    a = lax.all_gather(left, "col", axis=0, tiled=True)
    b = lax.all_gather(right, "row", axis=0, tiled=True)
    outer = lax.dot_general(a, b, (((0,), (0,)), ((), ())), precision=high) / S
    cut = outer.reshape(ti, C, tj, C)
    pair_out = jnp.einsum("icje,cez->ijz", cut, cube, precision=high) + b_out
    g = jnp.einsum("ijz,cez->icje", pair_grad, cube, precision=high)
    g = g.reshape(ti * C, tj * C)
    part = lax.dot_general(b, g, NT, precision=high) / S
    grad_left = lax.psum_scatter(part, "col", scatter_dimension=0, tiled=True)
    part = jnp.dot(a, g, precision=high) / S
    grad_right = lax.psum_scatter(part, "row", scatter_dimension=0, tiled=True)
    gw = jnp.einsum("icje,ijz->cez", cut, pair_grad, precision=high).reshape(C * C, Z)
    gw, gb = lax.psum((gw, jnp.sum(pair_grad, axis=(0, 1))), ("row", "col"))
    return (pair_out, grad_left, grad_right, gw / residues, gb / residues)


def body(left, right, w_out, b_out, pair_grad):
    tiles_fit = (right.shape[1] // C) % LANES == 0 and (left.shape[1] // C) % 4 == 0
    return (fast if tiles_fit else plain)(left, right, w_out, b_out, pair_grad)


def solution(mesh):
    placed = (P("col", "row"), P("row", "col"), P(), P(), P("row", "col", None))
    return jax.shard_map(
        body,
        mesh=mesh,
        in_specs=placed,
        out_specs=(P("row", "col", None), P("col", "row"), P("row", "col"), P(), P()),
        check_vma=False,
    )
```

time: 348 us -> 273 us (0.78)
  waiting for transfers between devices: 104 us -> 205 us
  matrix products: 86 us -> 0 us
  local copies, waits for them, and re-layouts: 89.2 us -> 8.22 us
  blocking collectives: 48.4 us -> 8.94 us
  Pallas kernels: 0 us -> 32.5 us
    psum x1, waiting for transfers between devices: 26.9 us -> 130 us  [fast(): total = lax.psum(jnp.concatenate([gw, gb8], axis=0), ('row', 'col'))]
    dot_general x6 -> x0, matrix products: 86 us -> none  [the longest x1 31.3 us: body(): jnp.einsum('icje,cez->ijz', outer_split, weight_cube, precision=highest)]
    unnamed x6 -> x4, waiting for transfers between devices: 77.5 us -> 0.57 us
    reduce_scatter x0 -> x2, waiting for transfers between devices: none -> 54.1 us  [the longest x1 42.2 us: fast(): grad_right = lax.psum_scatter(gr, 'row', scatter_dimension=0, tiled=True)]
    psum x1 -> x0, blocking collectives: 41.2 us -> none  [body(): grad_weight, grad_bias = lax.psum((weight_term, bias_term), ('row', 'col'))]
    reshape x2 -> x4, local copies, waits for them, and re-layouts: 44.7 us -> 5.21 us  [the longest x1 2.14 us: fast(): w = w_out.reshape(C, C, Z).transpose(1, 0, 2).reshape(C * C, Z)]
    pallas_call x0 -> x2, Pallas kernels: none -> 32.5 us  [the longest x1 19.5 us: fast(): pl.pallas_call(functools.partial(second_kernel, tj, scale), out_shape=[sh...]
    dot_general x1 -> x0, local copies, waits for them, and re-layouts: 21.8 us -> none  [body(): jnp.einsum('icje,ijz->cez', outer_split, pair_grad, precision=highest)]
  transfers between devices with their start and end apart: 4 -> 4, of which waited for: 3 -> 4; matrix products, arithmetic and copies ran while one was open for 34% -> 4% of each run, Pallas kernels for 0% -> 12%
where the time goes in v1:
time: 273 us
  waiting for transfers between devices  205 us (75%)
  Pallas kernels  32.5 us (12%)
  between operations  13.8 us (5%)
  blocking collectives  8.94 us (3%)
  local copies, waits for them, and re-layouts  8.22 us (3%)
  other arithmetic  3.73 us (1%)
    psum x1, waiting for transfers between devices, fast(): total = lax.psum(jnp.concatenate([gw, gb8], axis=0), ('row', 'col'))  130 us
    reduce_scatter x1, waiting for transfers between devices, fast(): grad_right = lax.psum_scatter(gr, 'row', scatter_dimension=0, tiled=True)  42.2 us
    all_gather x1, waiting for transfers between devices, fast(): b = lax.all_gather(mine, 'row', axis=0, tiled=True)  20.8 us
    pallas_call x1, Pallas kernels, fast(): pl.pallas_call(functools.partial(second_kernel, tj, scale), out_shape=[sh...  19.5 us
    pallas_call x1, Pallas kernels, fast(): pl.pallas_call(functools.partial(first_kernel, tj), out_shape=[shape((S,...  13 us
    reduce_scatter x1, waiting for transfers between devices, fast(): grad_left = lax.psum_scatter(part, 'col', scatter_dimension=0, tiled=True)  12 us
    all_gather x1, blocking collectives, fast(): a = lax.all_gather(left, 'col', axis=0, tiled=True)  8.94 us
  transfers between devices with their start and end apart: 4, of which 4 were waited for; matrix products, arithmetic and copies ran while one was open for 4% of the time, Pallas kernels for 12%

profile of v1, /device:TPU:0, one launch (start us, length us, event | category | flops | bytes accessed | tf_op | source)
XLA Modules:
  0.0 272.6 jit_solution(4572203779745348969)
XLA Ops:
  7.2 0.0 all-gather.2.cloned.1.call-start
  7.2 1.1 reshape.43
  8.3 0.8 copy.14
  9.1 0.0 all-gather.2.cloned.1.call-update
  9.1 0.0 reduce-scatter.5.cloned.1.call-start
  9.2 2.1 copy.15
  11.3 8.9 %all_gather.6.a = f32[128,512]{1,0:T(8,128)} all-gather(f32[64,512]{1,0:T(8,128)} %param.5), channel_id=1, replica_groups=mesh['row'=16,'col'=2] {'col'}, dimensions={0}, use_global_device_ids=true | all-gather | bytes 393216 | tf_op jit(solution)/shard_map/all_gather | solution.py:173
  20.3 13.0 %grads_of_outer.1 = (f32[128,4096]{1,0:T(8,128)}, bf16[512,4096]{1,0:T(8,128)(2,1)}, bf16[512,4096]{1,0:T(8,128)(2,1)}, bf16[2048,128]{1,0:T(8,128)(2,1)}, bf16[2048,128]{1,0:T(8,128)(2,1)}, /*index=5*/f32[1,128]{1,0:T(1,128)}) custom-call(f32[128,512]{1,0:T(8,128)} %all_gather.6.a, f32[2048,128]{1,0:T(8,128)} %bitcast.26, f32[1024,128]{1,0:T(8,128)} %bitcast.22), custom_call_target="tpu_custom_call" | custom-call | flops 3221225472 | bytes 16777216 | tf_op jit(solution)/shard_map/grads_of_outer/pallas_call | solution.py:177
  33.3 0.0 reduce-scatter.5.cloned.1.call-update
  33.3 0.0 all-reduce.2.cloned.1.call-start
  33.4 0.7 multiply_bitcast_fusion
  34.0 20.8 %all-gather.2.cloned.1.call-done.b = f32[128,4096]{1,0:T(8,128)} async-done(((f32[8,4096]{1,0:T(8,128)}), f32[128,4096]{1,0:T(8,128)}) %all-gather.2.cloned.1.call-update) | async-done | bytes 2097168 | tf_op jit(solution)/shard_map/all_gather | solution.py:174
  54.8 19.5 %outer_and_rest.1 = (f32[2048,128]{1,0:T(8,128)}, f32[128,512]{1,0:T(8,128)}, f32[1024,128]{1,0:T(8,128)}) custom-call(f32[128,512]{1,0:T(8,128)} %all_gather.6.a, f32[128,4096]{1,0:T(8,128)} %all-gather.2.cloned.1.call-done.b, f32[1024,128]{1,0:T(8,128)} %bitcast.23, f32[1,128]{1,0:T(1,128)} %bitcast.27, bf16[512,4096]{1,0:T(8,128)(2,1)} %get-tuple-element.14.gh, ...), custom_call_target="tpu_custom_call" | custom-call | flops 6442450944 | bytes 16777216 | tf_op jit(solution)/shard_map/outer_and_rest/pallas_call | solution.py:194
  74.3 1.9 pad_maximum_fusion
  76.2 0.0 all-reduce.2.cloned.1.call-update
  76.2 0.0 reduce-scatter.3.cloned.1.call-start
  76.2 0.5 reduce-scatter.3.cloned.1.call-update
  76.8 42.2 %reduce-scatter.5.cloned.1.call-done = f32[8,4096]{1,0:T(8,128)} async-done(((f32[128,4096]{1,0:T(8,128)}), f32[8,4096]{1,0:T(8,128)}) %reduce-scatter.5.cloned.1.call-update) | async-done | bytes 131088 | tf_op jit(solution)/shard_map/reduce_scatter | solution.py:193
  118.9 1.1 copy.16
  120.0 0.9 reshape.51
  120.9 129.8 %all-reduce.2.cloned.1.call-done = f32[1032,128]{1,0:T(8,128)} async-done(((f32[1032,128]{1,0:T(8,128)}), f32[1032,128]{1,0:T(8,128)}) %all-reduce.2.cloned.1.call-update) | async-done | bytes 528400 | tf_op jit(solution)/shard_map/psum | solution.py:215
  250.7 1.1 slice.8
  251.8 1.1 copy.17
  252.9 1.2 slice_reduce_fusion
  254.1 12.0 %reduce-scatter.3.cloned.1.call-done = f32[64,512]{1,0:T(8,128)} async-done(((f32[128,512]{1,0:T(8,128)}), f32[64,512]{1,0:T(8,128)}) %reduce-scatter.3.cloned.1.call-update) | async-done | bytes 131088 | tf_op jit(solution)/shard_map/reduce_scatter | solution.py:213
  (1 shorter events, 0.0 us)
Async XLA Ops:
  7.2 47.6 %all-gather.2.cloned.1.call-start = ((), (), s32[]{:S(2)}) async-start(), calls=%async_computation.2 | async-start | bytes 2228224 | tf_op jit(solution)/shard_map/all_gather | solution.py:174
  9.1 109.8 %reduce-scatter.5.cloned.1.call-start = ((), (), s32[]{:S(2)}) async-start(), calls=%async_computation.4 | async-start | bytes 2228224 | tf_op jit(solution)/shard_map/reduce_scatter | solution.py:193
  33.3 217.4 %all-reduce.2.cloned.1.call-start = ((), (), s32[]{:S(2)}) async-start(), calls=%async_computation.5 | async-start | bytes 1056768 | tf_op jit(solution)/shard_map/psum | solution.py:215
  76.2 189.9 %reduce-scatter.3.cloned.1.call-start = ((), (), s32[]{:S(2)}) async-start(), calls=%async_computation.3 | async-start | bytes 393216 | tf_op jit(solution)/shard_map/reduce_scatter | solution.py:213
Sparse Core Ops, SparseCore 0:
  10.7 44.0 all-gather.1
  58.5 60.3 reduce-scatter.4
  125.0 125.6 all-reduce.1
  253.3 12.6 reduce-scatter.2

commit v2 on v1

v2 whole, which is shorter than its diff:
```python
import functools

import jax
import jax.numpy as jnp
from jax import lax
from jax.experimental import pallas as pl
from jax.experimental.pallas import tpu as pltpu
from jax.sharding import PartitionSpec as P

C = 32
Z = 128
S = 128
LANES = 128
BF = jnp.bfloat16
F32 = jnp.float32
NN = (((1,), (0,)), ((), ()))
NT = (((1,), (1,)), ((), ()))


def split(x):
    high = x.astype(BF)
    return high, (x - high.astype(F32)).astype(BF)


def mm(a, b, dims):
    return lax.dot_general(a, b, dims, preferred_element_type=F32)


def bit_reverse(value, bits):
    return sum(((value >> k) & 1) << (bits - 1 - k) for k in range(bits))


def split_grad(pg, pgh, pgl):
    rows = pg.shape[0]
    step = min(rows, 512)

    def one(k, total):
        at = pl.ds(pl.multiple_of(k * step, step), step)
        x = pg[at, :]
        high, low = split(x)
        pgh[at, :] = high
        pgl[at, :] = low
        return total + jnp.sum(x.reshape(step // 8, 8, x.shape[1]), axis=0)

    return lax.fori_loop(0, rows // step, one, jnp.zeros((8, pg.shape[1]), F32))


def make_grad_outer(pgh, pgl, w, gh, gl, tj, first, last):
    wh, wl = split(w[...])
    both = jnp.concatenate([wh, wl], axis=1)
    group = 2

    def one(k, carry):
        at = pl.ds(pl.multiple_of(k * group * tj, group * tj), group * tj)
        ph, low = pgh[at, :], pgl[at, :]
        g = mm(both, jnp.concatenate([ph, ph], axis=1), NT) + mm(wh, low, NT)
        high, low = split(g)
        for i in range(group):
            rows = pl.ds(pl.multiple_of(k * group * C + i * C, C), C)
            for e in range(C):
                gh[rows, e * tj : (e + 1) * tj] = high[e * C : (e + 1) * C, i * tj : (i + 1) * tj]
                gl[rows, e * tj : (e + 1) * tj] = low[e * C : (e + 1) * C, i * tj : (i + 1) * tj]
        return carry

    lax.fori_loop(first, last, one, 0)


def make_grad_right(a, gh, gl, acc, width):
    n, rows, _ = acc.shape
    bits = n.bit_length() - 1
    ah, al = split(a * (1.0 / S))
    both = jnp.concatenate([ah, al], axis=0)

    def one(k, carry):
        cols = pl.ds(pl.multiple_of(k * width, width), width)
        high, low = gh[:, cols], gl[:, cols]
        r = mm(both, high, NN)
        r = r[:S] + r[S:] + mm(ah, low, NN)
        for p in range(n):
            acc[bit_reverse(p, bits), :, cols] = r[p * rows : (p + 1) * rows]
        return carry

    lax.fori_loop(0, gh.shape[1] // width, one, 0)


def split_right(raw, bh, bl, width):
    n = raw.shape[0]
    bits = n.bit_length() - 1

    def one(k, carry):
        cols = pl.ds(pl.multiple_of(k * width, width), width)
        x = jnp.concatenate([raw[bit_reverse(p, bits), :, cols] for p in range(n)], axis=0)
        high, low = split(x)
        bh[:, cols] = high
        bl[:, cols] = low
        return carry

    lax.fori_loop(0, bh.shape[1] // width, one, 0)


def make_outer(a, bh, bl, oh, ol, tj):
    ath, atl = split(a.T * (1.0 / S))
    both = jnp.concatenate([ath, atl], axis=1)
    ti = a.shape[1] // C
    group = 4
    width = group * tj

    def one(k, carry):
        cols = pl.ds(pl.multiple_of(k * width, width), width)
        high, low = bh[:, cols], bl[:, cols]
        o = mm(both, jnp.concatenate([high, high], axis=0), NN) + mm(ath, low, NN)
        high, low = split(o)
        for e in range(group):
            rows = pl.ds(pl.multiple_of(k * group * C + e * C, C), C)
            for i in range(ti):
                oh[rows, i * tj : (i + 1) * tj] = high[i * C : (i + 1) * C, e * tj : (e + 1) * tj]
                ol[rows, i * tj : (i + 1) * tj] = low[i * C : (i + 1) * C, e * tj : (e + 1) * tj]
        return carry

    lax.fori_loop(0, bh.shape[1] // width, one, 0)


def make_grad_weight(oh, ol, pgh, pgl, acc, column_sums, scale):
    slots, held, _ = acc.shape
    piece = held - 8
    group = 256 // piece
    step = group * piece

    def one(k, carry):
        rows = pl.ds(pl.multiple_of(k * step, step), step)
        ph = pgh[...]
        r = mm(oh[rows, :], jnp.concatenate([ph, pgl[...]], axis=1), NN)
        r = (r[:, :Z] + r[:, Z:] + mm(ol[rows, :], ph, NN)) * scale
        for g in range(group):
            acc[k * group + g, :piece, :] = r[g * piece : (g + 1) * piece]
            acc[k * group + g, piece:, :] = column_sums * scale
        return carry

    lax.fori_loop(0, slots // group, one, 0)


def make_pair_out(oh, ol, w, bias, out, width, first, last):
    wh, wl = split(w[...].T)
    both = jnp.concatenate([wh, wl], axis=0)

    def one(k, carry):
        cols = pl.ds(pl.multiple_of(k * width, width), width)
        r = mm(both, oh[:, cols], NN)
        r = r[:Z] + r[Z:] + mm(wh, ol[:, cols], NN)
        out[cols, :] = r.T + bias[...]
        return carry

    lax.fori_loop(first, last, one, 0)


def make_grad_left(bh, bl, gh, gl, part, first, last):
    both = jnp.concatenate([bh[...], bl[...]], axis=0)
    r = mm(both, gh[first:last, :], NT)
    r = (r[:S] + r[S:] + mm(bh[...], gl[first:last, :], NT)) * (1.0 / S)
    half = part.shape[1]
    for h in range(2):
        part[h, :, first:last] = r[h * half : (h + 1) * half]


def kernel(
    n, tj, scale, left, mine, pg, w, bias, out, grad_left, grad_right, grad_weight, grad_bias,
    a_raw, b_raw, r_acc, r_in, l_part, l_in, w_acc, w_in, w_all, pgh, pgl, gh, gl, bh, bl, oh, ol,
    sent, got,
):
    row, col = lax.axis_index("row"), lax.axis_index("col")
    bits = n.bit_length() - 1
    row_bit = [(row // (1 << k)) % 2 for k in range(bits)]
    partner = [(row + (1 << k) * (1 - 2 * row_bit[k]), col) for k in range(bits)]
    across = (row, 1 - col)
    slot = sum(row_bit[k] * (1 << (bits - 1 - k)) for k in range(bits))
    order = partner[:2] + [across] + partner[2:]
    order_bit = row_bit[:2] + [col] + row_bit[2:]
    levels = len(order)
    w_slot = sum(order_bit[u] * (1 << (levels - 1 - u)) for u in range(levels))

    barrier = pltpu.get_barrier_semaphore()
    for device in order:
        pl.semaphore_signal(
            barrier, inc=1, device_id=device, device_id_type=pl.DeviceIdType.MESH
        )
    pl.semaphore_wait(barrier, levels)

    used = []

    def send(src, dst, device):
        k = len(used)
        used.append(k)
        copy = pltpu.make_async_remote_copy(
            src_ref=src,
            dst_ref=dst,
            send_sem=sent.at[k],
            recv_sem=got.at[k],
            device_id=device,
            device_id_type=pl.DeviceIdType.MESH,
        )
        copy.start()
        return copy

    def gather(buffer, place, t, device):
        window = pl.ds((place // (1 << t)) * (1 << t), 1 << t)
        return send(buffer.at[window], buffer.at[window], device)

    def scatter(acc, into, place, q, device):
        keep = (place // (1 << q)) * (1 << q)
        away = keep + (1 << q) * (1 - 2 * ((place // (1 << q)) % 2))
        return send(acc.at[pl.ds(away, 1 << q)], into.at[pl.ds(1 << q, 1 << q)], device)

    def add(acc, into, place, q):
        keep = (place // (1 << q)) * (1 << q)

        def one(k, carry):
            acc[keep + k] = acc[keep + k] + into[(1 << q) + k]
            return carry

        lax.fori_loop(0, 1 << q, one, 0)

    def next_right(t):
        return gather(b_raw, slot, t, partner[bits - 1 - t])

    def next_scatter(u):
        return scatter(r_acc, r_in, slot, bits - 1 - u, partner[u])

    def next_weight(u):
        return scatter(w_acc, w_in, w_slot, levels - 1 - u, order[u])

    a_raw[col] = left[...]
    b_raw[slot] = mine[...]
    right_copy = next_right(0)
    left_copy = send(a_raw.at[col], a_raw.at[col], across)

    column_sums = split_grad(pg, pgh, pgl)
    groups = pgh.shape[0] // (2 * tj)
    cut = groups // 4
    make_grad_outer(pgh, pgl, w, gh, gl, tj, 0, cut)
    for t in range(1, bits - 1):
        right_copy.wait()
        right_copy = next_right(t)
        if t == 1:
            make_grad_outer(pgh, pgl, w, gh, gl, tj, cut, groups)
    left_copy.wait()
    a = jnp.concatenate([a_raw[0], a_raw[1]], axis=0)
    make_grad_right(a, gh, gl, r_acc, 4 * tj)
    r_copy = next_scatter(0)
    r_copy.wait()
    add(r_acc, r_in, slot, bits - 1)
    r_copy = next_scatter(1)
    right_copy.wait()
    right_copy = next_right(bits - 1)
    right_copy.wait()

    split_right(b_raw, bh, bl, 4 * tj)
    make_outer(a, bh, bl, oh, ol, tj)
    r_copy.wait()
    add(r_acc, r_in, slot, bits - 2)
    r_copy = next_scatter(2)
    make_grad_weight(oh, ol, pgh, pgl, w_acc, column_sums, scale)
    w_copy = next_weight(0)
    size = gh.shape[0] // 2
    make_grad_left(bh, bl, gh, gl, l_part, 0, size)
    w_copy.wait()
    add(w_acc, w_in, w_slot, levels - 1)
    w_copy = next_weight(1)
    r_copy.wait()
    add(r_acc, r_in, slot, bits - 3)
    for u in range(3, bits):
        r_copy = next_scatter(u)
        if u == 3:
            make_grad_left(bh, bl, gh, gl, l_part, size, 2 * size)
            left_copy = send(l_part.at[1 - col], l_in, across)
        if u < bits - 1:
            r_copy.wait()
            add(r_acc, r_in, slot, bits - 1 - u)
    steps = pgh.shape[0] // (2 * tj)
    parts = 2 * levels - 2
    at = [steps * k // parts for k in range(parts + 1)]

    def some_out(k):
        if at[k] < at[k + 1]:
            make_pair_out(oh, ol, w, bias, out, 2 * tj, at[k], at[k + 1])

    for u in range(1, levels):
        some_out(u - 1)
        w_copy.wait()
        add(w_acc, w_in, w_slot, levels - 1 - u)
        if u < levels - 1:
            w_copy = next_weight(u + 1)
        if u == 2:
            r_copy.wait()
            add(r_acc, r_in, slot, 0)
            grad_right[...] = r_acc[slot]
    piece = w_all.shape[1]
    w_all[w_slot] = w_acc[w_slot, :piece, :]
    grad_bias[...] = jnp.sum(w_acc[w_slot, piece:, :], axis=0, keepdims=True)
    for t in range(levels):
        w_copy = gather(w_all, w_slot, t, order[levels - 1 - t])
        if t < levels - 1:
            some_out(levels - 1 + t)
        else:
            left_copy.wait()
            grad_left[...] = l_part[col] + l_in[...]
        w_copy.wait()
    grad_weight[...] = w_all[...]


def fast(left, right, w_out, b_out, pair_grad):
    ti = left.shape[1] // C
    tj = right.shape[1] // C
    pairs = ti * tj
    n = lax.axis_size("row")
    devices = n * lax.axis_size("col")
    piece = C * C // devices
    bits = n.bit_length() - 1
    copies = 2 * bits + 2 * (bits + 1) + 2
    vmem = pl.BlockSpec(memory_space=pltpu.VMEM)
    w = w_out.reshape(C, C, Z).transpose(1, 0, 2).reshape(C * C, Z)
    mine = right.reshape(-1, tj, C).transpose(0, 2, 1).reshape(right.shape)
    shape = jax.ShapeDtypeStruct
    scratch = [
        ((2,) + left.shape, F32),
        ((n,) + right.shape, F32),
        ((n,) + right.shape, F32),
        ((n,) + right.shape, F32),
        ((2,) + left.shape, F32),
        (left.shape, F32),
        ((devices, piece + 8, Z), F32),
        ((devices, piece + 8, Z), F32),
        ((devices, piece, Z), F32),
        ((pairs, Z), BF),
        ((pairs, Z), BF),
        ((ti * C, C * tj), BF),
        ((ti * C, C * tj), BF),
        ((S, C * tj), BF),
        ((S, C * tj), BF),
        ((C * C, pairs), BF),
        ((C * C, pairs), BF),
    ]
    out, grad_left, grad_right, gw, gb = pl.pallas_call(
        functools.partial(kernel, n, tj, 1.0 / (ti * n)),
        out_shape=[
            shape((pairs, Z), F32),
            shape(left.shape, F32),
            shape(right.shape, F32),
            shape((devices, piece, Z), F32),
            shape((1, Z), F32),
        ],
        in_specs=[vmem] * 5,
        out_specs=[vmem] * 5,
        scratch_shapes=[pltpu.VMEM(*s) for s in scratch]
        + [pltpu.SemaphoreType.DMA((copies,)), pltpu.SemaphoreType.DMA((copies,))],
        compiler_params=pltpu.CompilerParams(
            vmem_limit_bytes=56 * 1024 * 1024, collective_id=0, has_side_effects=True
        ),
        cost_estimate=pl.CostEstimate(
            flops=36 * pairs * C * C * Z, bytes_accessed=1 << 23, transcendentals=0
        ),
        name="outer_product_mean",
    )(left, mine, pair_grad.reshape(pairs, Z), w, b_out.reshape(1, Z))
    grad_weight = gw.reshape(C, C, Z).transpose(1, 0, 2).reshape(C * C, Z)
    grad_right = grad_right.reshape(-1, C, tj).transpose(0, 2, 1).reshape(right.shape)
    return (out.reshape(pair_grad.shape), grad_left, grad_right, grad_weight, gb.reshape(Z))


def plain(left, right, w_out, b_out, pair_grad):
    high = lax.Precision.HIGHEST
    ti = left.shape[1] // C
    tj = right.shape[1] // C
    residues = ti * lax.axis_size("row")
    cube = w_out.reshape(C, C, Z)
    a = lax.all_gather(left, "col", axis=0, tiled=True)
    b = lax.all_gather(right, "row", axis=0, tiled=True)
    outer = lax.dot_general(a, b, (((0,), (0,)), ((), ())), precision=high) / S
    cut = outer.reshape(ti, C, tj, C)
    pair_out = jnp.einsum("icje,cez->ijz", cut, cube, precision=high) + b_out
    g = jnp.einsum("ijz,cez->icje", pair_grad, cube, precision=high)
    g = g.reshape(ti * C, tj * C)
    part = lax.dot_general(b, g, NT, precision=high) / S
    grad_left = lax.psum_scatter(part, "col", scatter_dimension=0, tiled=True)
    part = jnp.dot(a, g, precision=high) / S
    grad_right = lax.psum_scatter(part, "row", scatter_dimension=0, tiled=True)
    gw = jnp.einsum("icje,ijz->cez", cut, pair_grad, precision=high).reshape(C * C, Z)
    gw, gb = lax.psum((gw, jnp.sum(pair_grad, axis=(0, 1))), ("row", "col"))
    return (pair_out, grad_left, grad_right, gw / residues, gb / residues)


def body(left, right, w_out, b_out, pair_grad):
    n, m = lax.axis_size("row"), lax.axis_size("col")
    fits = (
        (right.shape[1] // C) % LANES == 0
        and (left.shape[1] // C) % 8 == 0
        and m == 2
        and n >= 16
        and n & (n - 1) == 0
        and right.shape[0] % 8 == 0
        and (C * C) % (8 * n * m) == 0
    )
    return (fast if fits else plain)(left, right, w_out, b_out, pair_grad)


def solution(mesh):
    placed = (P("col", "row"), P("row", "col"), P(), P(), P("row", "col", None))
    return jax.shard_map(
        body,
        mesh=mesh,
        in_specs=placed,
        out_specs=(P("row", "col", None), P("col", "row"), P("row", "col"), P(), P()),
        check_vma=False,
    )
```

time: 273 us -> 88.7 us (0.32)
  waiting for transfers between devices: 205 us -> 0 us
  Pallas kernels: 32.5 us -> 79.3 us
  between operations: 13.8 us -> 0.69 us
  blocking collectives: 8.94 us -> 0 us
  other arithmetic: 3.73 us -> 0 us
    psum x1 -> x0, waiting for transfers between devices: 130 us -> none  [fast(): total = lax.psum(jnp.concatenate([gw, gb8], axis=0), ('row', 'col'))]
    reduce_scatter x2 -> x0, waiting for transfers between devices: 54.1 us -> none  [the longest x1 42.2 us: fast(): grad_right = lax.psum_scatter(gr, 'row', scatter_dimension=0, tiled=True)]
    pallas_call x2 -> x1, Pallas kernels: 32.5 us -> 79.3 us  [fast(): pl.pallas_call(functools.partial(kernel, n, tj, 1.0 / (ti * n)), out_shap...]
    all_gather x1 -> x0, waiting for transfers between devices: 20.8 us -> none  [fast(): b = lax.all_gather(mine, 'row', axis=0, tiled=True)]
    all_gather x1 -> x0, blocking collectives: 8.94 us -> none  [fast(): a = lax.all_gather(left, 'col', axis=0, tiled=True)]
  transfers between devices with their start and end apart: 4 -> 0, of which waited for: 4 -> 0; matrix products, arithmetic and copies ran while one was open for 4% -> 0% of each run, Pallas kernels for 12% -> 0%
where the time goes in v2:
time: 88.7 us; the launch traced here: 88.4 us
  Pallas kernels  79.3 us (89%)
  local copies, waits for them, and re-layouts  8.48 us (10%)
    pallas_call x1, Pallas kernels, fast(): pl.pallas_call(functools.partial(kernel, n, tj, 1.0 / (ti * n)), out_shap...  79.3 us
    unnamed x13, local copies, waits for them, and re-layouts  2.2 us
    reshape x2, local copies, waits for them, and re-layouts, fast(): grad_right.reshape(-1, C, tj).transpose(0, 2, 1).reshape(right.shape)  2.11 us

profile of v2, /device:TPU:0, one launch (start us, length us, event | category | flops | bytes accessed | tf_op | source)
XLA Modules:
  0.0 88.4 jit_solution(3571965165735686852)
XLA Ops:
  0.6 0.0 copy-start.1
  0.6 1.1 %reshape.43 = f32[8,128,32]{2,1,0:T(8,128)S(1)} reshape(f32[8,4096]{1,0:T(8,128)} %param.6) | data formatting | bytes 262144 | tf_op jit(solution)/shard_map/reshape | solution.py:321
  1.8 0.8 copy.13
  2.6 0.0 copy-done.1
  2.6 1.1 %copy.14 = f32[32,32,128]{2,0,1:T(8,128)} copy(f32[32,32,128]{2,1,0:T(8,128)S(1)} %bitcast.17) | data formatting | bytes 1048576 | tf_op jit(solution)/shard_map/reshape | solution.py:320
  3.7 79.3 %outer_product_mean.1 = (f32[2048,128]{1,0:T(8,128)}, f32[64,512]{1,0:T(8,128)}, f32[8,4096]{1,0:T(8,128)}, f32[32,32,128]{2,1,0:T(8,128)}, f32[1,128]{1,0:T(1,128)}) custom-call(f32[64,512]{1,0:T(8,128)} %left.1, f32[8,4096]{1,0:T(8,128)} %bitcast.21, f32[2048,128]{1,0:T(8,128)} %bitcast.23, f32[1024,128]{1,0:T(8,128)} %bitcast.20, f32[1,128]{1,0:T(1,128)} %bitcast.24), custom_call_target="tpu_custom_call" | custom-call | flops 9663676416 | bytes 8388608 | tf_op jit(solution)/shard_map/outer_product_mean/pallas_call | solution.py:342
  83.0 0.0 copy-start.2
  83.0 0.0 copy-start
  83.0 1.2 %copy.15 = f32[8,32,128]{1,2,0:T(8,128)S(1)} copy(f32[8,32,128]{2,0,1:T(8,128)} %bitcast.22) | data formatting | bytes 262144 | tf_op jit(solution)/shard_map/reshape | solution.py:364
  84.3 0.9 %reshape.51 = f32[8,4096]{1,0:T(8,128)} reshape(f32[8,128,32]{2,1,0:T(8,128)S(1)} %bitcast.14) | data formatting | bytes 262144 | tf_op jit(solution)/shard_map/reshape | solution.py:364
  85.1 0.0 copy-done.2
  85.1 1.1 %copy.16 = f32[32,32,128]{2,1,0:T(8,128)} copy(f32[32,32,128]{2,0,1:T(8,128)S(1)} %bitcast.19) | data formatting | bytes 1048576 | tf_op jit(solution)/shard_map/transpose | solution.py:363
  86.2 0.0 copy-done
  86.3 0.0 copy-start.3
  86.3 1.0 %copy.20 = f32[16,128,128]{2,1,0:T(8,128)} copy(f32[16,128,128]{2,1,0:T(8,128)S(1)} %bitcast.16) | data formatting | bytes 2097152
  87.2 0.1 copy-done.3
  87.3 0.0 copy-start.4
  87.3 0.7 copy.21
  87.9 0.0 copy-done.4
  87.9 0.5 copy.22
Async XLA Ops:
  0.6 2.0 %copy-start.1 = (f32[1024,128]{1,0:T(8,128)S(1)}, f32[1024,128]{1,0:T(8,128)}, u32[]{:S(2)}) copy-start(f32[1024,128]{1,0:T(8,128)} %param.7) | copy-start | bytes 1572868
  83.0 2.1 %copy-start.2 = (f32[32,32,128]{2,1,0:T(8,128)S(1)}, f32[32,32,128]{2,1,0:T(8,128)}, u32[]{:S(2)}) copy-start(f32[32,32,128]{2,1,0:T(8,128)} %get-tuple-element.13) | copy-start | bytes 1572868
  83.0 3.2 %copy-start = (f32[2048,128]{1,0:T(8,128)S(1)}, f32[2048,128]{1,0:T(8,128)}, u32[]{:S(2)}) copy-start(f32[2048,128]{1,0:T(8,128)} %get-tuple-element.10) | copy-start | bytes 3145732
  86.3 1.0 %copy-start.3 = (f32[64,512]{1,0:T(8,128)S(1)}, f32[64,512]{1,0:T(8,128)}, u32[]{:S(2)}) copy-start(f32[64,512]{1,0:T(8,128)} %get-tuple-element.21) | copy-start | bytes 393220
  87.3 0.7 copy-start.4

commit v3 on v2

--- a/solution.py
+++ b/solution.py
@@ -83,19 +83,19 @@
     lax.fori_loop(0, gh.shape[1] // width, one, 0)
 
 
-def split_right(raw, bh, bl, width):
+def split_right(raw, steps, bh, bl, base, width):
     n = raw.shape[0]
-    bits = n.bit_length() - 1
+    slots = [sum(((p >> k) & 1) << t for t, k in enumerate(steps)) for p in range(n)]
 
     def one(k, carry):
         cols = pl.ds(pl.multiple_of(k * width, width), width)
-        x = jnp.concatenate([raw[bit_reverse(p, bits), :, cols] for p in range(n)], axis=0)
-        high, low = split(x)
-        bh[:, cols] = high
-        bl[:, cols] = low
-        return carry
-
-    lax.fori_loop(0, bh.shape[1] // width, one, 0)
+        to = pl.ds(pl.multiple_of(base + k * width, width), width)
+        high, low = split(jnp.concatenate([raw[slot, :, cols] for slot in slots], axis=0))
+        bh[:, to] = high
+        bl[:, to] = low
+        return carry
+
+    lax.fori_loop(0, raw.shape[2] // width, one, 0)
 
 
 def make_outer(a, bh, bl, oh, ol, tj):
@@ -120,13 +120,14 @@
     lax.fori_loop(0, bh.shape[1] // width, one, 0)
 
 
-def make_grad_weight(oh, ol, pgh, pgl, acc, column_sums, scale):
+def make_grad_weight(oh, ol, pgh, pgl, acc, column_sums, scale, half):
     slots, held, _ = acc.shape
     piece = held - 8
     group = 256 // piece
     step = group * piece
 
-    def one(k, carry):
+    def one(turn, carry):
+        k = half * (slots // group // 2) + turn
         rows = pl.ds(pl.multiple_of(k * step, step), step)
         ph = pgh[...]
         r = mm(oh[rows, :], jnp.concatenate([ph, pgl[...]], axis=1), NN)
@@ -136,7 +137,7 @@
             acc[k * group + g, piece:, :] = column_sums * scale
         return carry
 
-    lax.fori_loop(0, slots // group, one, 0)
+    lax.fori_loop(0, slots // group // 2, one, 0)
 
 
 def make_pair_out(oh, ol, w, bias, out, width, first, last):
@@ -163,8 +164,8 @@
 
 
 def kernel(
-    n, tj, scale, left, mine, pg, w, bias, out, grad_left, grad_right, grad_weight, grad_bias,
-    a_raw, b_raw, r_acc, r_in, l_part, l_in, w_acc, w_in, w_all, pgh, pgl, gh, gl, bh, bl, oh, ol,
+    n, tj, scale, left, mine, pg, w_cube, bias, out, grad_left, grad_right, grad_weight, grad_bias,
+    a_raw, b_one, b_two, r_acc, r_in, l_part, l_in, w_acc, w_in, w_all, w, pgh, pgl, gh, gl, bh, bl, oh, ol,
     sent, got,
 ):
     row, col = lax.axis_index("row"), lax.axis_index("col")
@@ -177,13 +178,30 @@
     order_bit = row_bit[:2] + [col] + row_bit[2:]
     levels = len(order)
     w_slot = sum(order_bit[u] * (1 << (levels - 1 - u)) for u in range(levels))
+    group = 1 << (levels - 2)
+    others = []
+    for d in range(1, group):
+        other_row, other_col, other_slot = row, col, w_slot
+        for u in range(2, levels):
+            weight = 1 << (levels - 1 - u)
+            if d & weight:
+                other_slot = other_slot + weight * (1 - 2 * order_bit[u])
+                if u == 2:
+                    other_col = 1 - col
+                else:
+                    other_row = other_row + (1 << (u - 1)) * (1 - 2 * order_bit[u])
+        others.append((d, (other_row, other_col), other_slot))
+    steps_one = [*range(bits - 1, -1, -1)]
+    steps_two = [1, *range(bits - 1, 1, -1), 0]
+    slot_two = sum(row_bit[k] * (1 << t) for t, k in enumerate(steps_two))
 
     barrier = pltpu.get_barrier_semaphore()
-    for device in order:
+    greeted = order[:2] + [device for _, device, _ in others]
+    for device in greeted:
         pl.semaphore_signal(
             barrier, inc=1, device_id=device, device_id_type=pl.DeviceIdType.MESH
         )
-    pl.semaphore_wait(barrier, levels)
+    pl.semaphore_wait(barrier, len(greeted))
 
     used = []
 
@@ -220,7 +238,14 @@
         lax.fori_loop(0, 1 << q, one, 0)
 
     def next_right(t):
-        return gather(b_raw, slot, t, partner[bits - 1 - t])
+        return (
+            gather(b_one, slot, t, partner[steps_one[t]]),
+            gather(b_two, slot_two, t, partner[steps_two[t]]),
+        )
+
+    def await_right(copies):
+        for copy in copies:
+            copy.wait()
 
     def next_scatter(u):
         return scatter(r_acc, r_in, slot, bits - 1 - u, partner[u])
@@ -228,83 +253,85 @@
     def next_weight(u):
         return scatter(w_acc, w_in, w_slot, levels - 1 - u, order[u])
 
+    half_cols = b_one.shape[2]
     a_raw[col] = left[...]
-    b_raw[slot] = mine[...]
+    b_one[slot] = mine[:, :half_cols]
+    b_two[slot_two] = mine[:, half_cols:]
     right_copy = next_right(0)
     left_copy = send(a_raw.at[col], a_raw.at[col], across)
 
+    for e in range(C):
+        w[e * C : (e + 1) * C, :] = w_cube[:, e, :]
     column_sums = split_grad(pg, pgh, pgl)
     groups = pgh.shape[0] // (2 * tj)
-    cut = groups // 4
-    make_grad_outer(pgh, pgl, w, gh, gl, tj, 0, cut)
+    cuts = [groups // 8 + k * (groups - groups // 8) // (bits - 2) for k in range(bits - 1)]
+    make_grad_outer(pgh, pgl, w, gh, gl, tj, 0, cuts[0])
     for t in range(1, bits - 1):
-        right_copy.wait()
+        await_right(right_copy)
         right_copy = next_right(t)
-        if t == 1:
-            make_grad_outer(pgh, pgl, w, gh, gl, tj, cut, groups)
+        make_grad_outer(pgh, pgl, w, gh, gl, tj, cuts[t - 1], cuts[t])
     left_copy.wait()
     a = jnp.concatenate([a_raw[0], a_raw[1]], axis=0)
     make_grad_right(a, gh, gl, r_acc, 4 * tj)
     r_copy = next_scatter(0)
+    await_right(right_copy)
+    right_copy = next_right(bits - 1)
     r_copy.wait()
     add(r_acc, r_in, slot, bits - 1)
     r_copy = next_scatter(1)
-    right_copy.wait()
-    right_copy = next_right(bits - 1)
-    right_copy.wait()
-
-    split_right(b_raw, bh, bl, 4 * tj)
+    await_right(right_copy)
+
+    split_right(b_one, steps_one, bh, bl, 0, 4 * tj)
+    split_right(b_two, steps_two, bh, bl, half_cols, 4 * tj)
     make_outer(a, bh, bl, oh, ol, tj)
     r_copy.wait()
     add(r_acc, r_in, slot, bits - 2)
     r_copy = next_scatter(2)
-    make_grad_weight(oh, ol, pgh, pgl, w_acc, column_sums, scale)
+    make_grad_weight(oh, ol, pgh, pgl, w_acc, column_sums, scale, 1 - order_bit[0])
     w_copy = next_weight(0)
-    size = gh.shape[0] // 2
-    make_grad_left(bh, bl, gh, gl, l_part, 0, size)
+    make_grad_weight(oh, ol, pgh, pgl, w_acc, column_sums, scale, order_bit[0])
     w_copy.wait()
     add(w_acc, w_in, w_slot, levels - 1)
     w_copy = next_weight(1)
+    for u in range(3, bits):
+        r_copy.wait()
+        add(r_acc, r_in, slot, bits - u)
+        r_copy = next_scatter(u)
+    size = gh.shape[0] // 2
+    make_grad_left(bh, bl, gh, gl, l_part, 0, size)
+    make_grad_left(bh, bl, gh, gl, l_part, size, 2 * size)
+    left_copy = send(l_part.at[1 - col], l_in, across)
+    w_copy.wait()
+    add(w_acc, w_in, w_slot, levels - 2)
+    exchanged = [send(w_acc.at[to], w_in.at[d], device) for d, device, to in others]
+    at = [groups * k // 8 for k in (0, 3, 5, 8)]
+    make_pair_out(oh, ol, w, bias, out, 2 * tj, at[0], at[1])
+    for copy in exchanged:
+        copy.wait()
+    terms = [w_acc[w_slot]] + [w_in[d] for d, _, _ in others]
+    while len(terms) > 1:
+        terms = [one + two for one, two in zip(terms[::2], terms[1::2])]
+    total = terms[0]
+    piece = w_all.shape[1]
+    w_all[w_slot] = total[:piece]
+    spread = [send(w_all.at[w_slot], w_all.at[w_slot], device) for _, device, _ in others]
+    grad_bias[...] = jnp.sum(total[piece:], axis=0, keepdims=True)
+    make_pair_out(oh, ol, w, bias, out, 2 * tj, at[1], at[2])
+    for copy in spread:
+        copy.wait()
+    w_copy = gather(w_all, w_slot, levels - 2, order[1])
+    make_pair_out(oh, ol, w, bias, out, 2 * tj, at[2], at[3])
+    w_copy.wait()
+    w_copy = gather(w_all, w_slot, levels - 1, order[0])
     r_copy.wait()
-    add(r_acc, r_in, slot, bits - 3)
-    for u in range(3, bits):
-        r_copy = next_scatter(u)
-        if u == 3:
-            make_grad_left(bh, bl, gh, gl, l_part, size, 2 * size)
-            left_copy = send(l_part.at[1 - col], l_in, across)
-        if u < bits - 1:
-            r_copy.wait()
-            add(r_acc, r_in, slot, bits - 1 - u)
-    steps = pgh.shape[0] // (2 * tj)
-    parts = 2 * levels - 2
-    at = [steps * k // parts for k in range(parts + 1)]
-
-    def some_out(k):
-        if at[k] < at[k + 1]:
-            make_pair_out(oh, ol, w, bias, out, 2 * tj, at[k], at[k + 1])
-
-    for u in range(1, levels):
-        some_out(u - 1)
-        w_copy.wait()
-        add(w_acc, w_in, w_slot, levels - 1 - u)
-        if u < levels - 1:
-            w_copy = next_weight(u + 1)
-        if u == 2:
-            r_copy.wait()
-            add(r_acc, r_in, slot, 0)
-            grad_right[...] = r_acc[slot]
-    piece = w_all.shape[1]
-    w_all[w_slot] = w_acc[w_slot, :piece, :]
-    grad_bias[...] = jnp.sum(w_acc[w_slot, piece:, :], axis=0, keepdims=True)
-    for t in range(levels):
-        w_copy = gather(w_all, w_slot, t, order[levels - 1 - t])
-        if t < levels - 1:
-            some_out(levels - 1 + t)
-        else:
-            left_copy.wait()
-            grad_left[...] = l_part[col] + l_in[...]
-        w_copy.wait()
-    grad_weight[...] = w_all[...]
+    add(r_acc, r_in, slot, 0)
+    grad_right[...] = r_acc[slot]
+    left_copy.wait()
+    grad_left[...] = l_part[col] + l_in[...]
+    w_copy.wait()
+    m = C // piece
+    for e in range(C):
+        grad_weight[:, e, :] = w_all[e * m : (e + 1) * m].reshape(C, w_all.shape[2])
 
 
 def fast(left, right, w_out, b_out, pair_grad):
@@ -315,14 +342,15 @@
     devices = n * lax.axis_size("col")
     piece = C * C // devices
     bits = n.bit_length() - 1
-    copies = 2 * bits + 2 * (bits + 1) + 2
+    copies = 3 * bits + 6 + 2 * (n // 2 - 1)
     vmem = pl.BlockSpec(memory_space=pltpu.VMEM)
-    w = w_out.reshape(C, C, Z).transpose(1, 0, 2).reshape(C * C, Z)
+    half = (n, right.shape[0], right.shape[1] // 2)
     mine = right.reshape(-1, tj, C).transpose(0, 2, 1).reshape(right.shape)
     shape = jax.ShapeDtypeStruct
     scratch = [
         ((2,) + left.shape, F32),
-        ((n,) + right.shape, F32),
+        (half, F32),
+        (half, F32),
         ((n,) + right.shape, F32),
         ((n,) + right.shape, F32),
         ((2,) + left.shape, F32),
@@ -330,6 +358,7 @@
         ((devices, piece + 8, Z), F32),
         ((devices, piece + 8, Z), F32),
         ((devices, piece, Z), F32),
+        ((C * C, Z), F32),
         ((pairs, Z), BF),
         ((pairs, Z), BF),
         ((ti * C, C * tj), BF),
@@ -345,7 +374,7 @@
             shape((pairs, Z), F32),
             shape(left.shape, F32),
             shape(right.shape, F32),
-            shape((devices, piece, Z), F32),
+            shape((C, C, Z), F32),
             shape((1, Z), F32),
         ],
         in_specs=[vmem] * 5,
@@ -359,8 +388,8 @@
             flops=36 * pairs * C * C * Z, bytes_accessed=1 << 23, transcendentals=0
         ),
         name="outer_product_mean",
-    )(left, mine, pair_grad.reshape(pairs, Z), w, b_out.reshape(1, Z))
-    grad_weight = gw.reshape(C, C, Z).transpose(1, 0, 2).reshape(C * C, Z)
+    )(left, mine, pair_grad.reshape(pairs, Z), w_out.reshape(C, C, Z), b_out.reshape(1, Z))
+    grad_weight = gw.reshape(C * C, Z)
     grad_right = grad_right.reshape(-1, C, tj).transpose(0, 2, 1).reshape(right.shape)
     return (out.reshape(pair_grad.shape), grad_left, grad_right, grad_weight, gb.reshape(Z))
 

time: 88.7 us -> 77 us (0.87)
  Pallas kernels: 79.3 us -> 69.2 us
  local copies, waits for them, and re-layouts: 8.48 us -> 6.95 us
    pallas_call x1, Pallas kernels: 79.3 us -> 69.2 us  [fast(): pl.pallas_call(functools.partial(kernel, n, tj, 1.0 / (ti * n)), out_shap...]
    reshape x1 -> x0, local copies, waits for them, and re-layouts: 1.1 us -> none  [fast(): w = w_out.reshape(C, C, Z).transpose(1, 0, 2).reshape(C * C, Z)]
    transpose x1 -> x0, local copies, waits for them, and re-layouts: 1.1 us -> none  [fast(): grad_weight = gw.reshape(C, C, Z).transpose(1, 0, 2).reshape(C * C, Z)]
    unnamed x13 -> x12, local copies, waits for them, and re-layouts: 2.2 us -> 2.97 us
where the time goes in v3:
time: 77 us; the launch traced here: 76.8 us
  Pallas kernels  69.2 us (90%)
  local copies, waits for them, and re-layouts  6.95 us (9%)
    pallas_call x1, Pallas kernels, fast(): pl.pallas_call(functools.partial(kernel, n, tj, 1.0 / (ti * n)), out_shap...  69.2 us
    unnamed x12, local copies, waits for them, and re-layouts  2.97 us
    reshape x2, local copies, waits for them, and re-layouts, fast(): grad_right.reshape(-1, C, tj).transpose(0, 2, 1).reshape(right.shape)  2.08 us

profile of v3, /device:TPU:0, one launch (start us, length us, event | category | flops | bytes accessed | tf_op | source)
XLA Modules:
  0.0 76.8 jit_solution(12977932119173281548)
XLA Ops:
  0.6 1.1 %reshape.40 = f32[8,128,32]{2,1,0:T(8,128)S(1)} reshape(f32[8,4096]{1,0:T(8,128)} %param.6) | data formatting | bytes 262144 | tf_op jit(solution)/shard_map/reshape | solution.py:348
  1.7 0.8 %copy.12 = f32[8,32,128]{2,0,1:T(8,128)} copy(f32[8,32,128]{1,2,0:T(8,128)S(1)} %bitcast.11) | data formatting | bytes 262144 | tf_op jit(solution)/shard_map/transpose | solution.py:348
  2.5 69.2 %outer_product_mean.1 = (f32[2048,128]{1,0:T(8,128)}, f32[64,512]{1,0:T(8,128)}, f32[8,4096]{1,0:T(8,128)}, f32[32,32,128]{2,1,0:T(8,128)}, f32[1,128]{1,0:T(1,128)}) custom-call(f32[64,512]{1,0:T(8,128)} %left.1, f32[8,4096]{1,0:T(8,128)} %bitcast.14, f32[2048,128]{1,0:T(8,128)} %bitcast.16, f32[32,32,128]{2,1,0:T(8,128)} %bitcast.17, f32[1,128]{1,0:T(1,128)} %bitcast.18), custom_call_target="tpu_custom_call" | custom-call | flops 9663676416 | bytes 8388608 | tf_op jit(solution)/shard_map/outer_product_mean/pallas_call | solution.py:371
  71.8 0.0 copy-start
  71.8 1.2 %copy.13 = f32[8,32,128]{1,2,0:T(8,128)S(1)} copy(f32[8,32,128]{2,0,1:T(8,128)} %bitcast.15) | data formatting | bytes 262144 | tf_op jit(solution)/shard_map/reshape | solution.py:393
  73.0 0.9 %reshape.47 = f32[8,4096]{1,0:T(8,128)} reshape(f32[8,128,32]{2,1,0:T(8,128)S(1)} %bitcast.10) | data formatting | bytes 262144 | tf_op jit(solution)/shard_map/reshape | solution.py:393
  73.9 0.0 copy-done
  73.9 0.0 copy-start.2
  73.9 0.0 copy-start.1
  73.9 1.0 %copy.18 = f32[16,128,128]{2,1,0:T(8,128)} copy(f32[16,128,128]{2,1,0:T(8,128)S(1)} %bitcast.12) | data formatting | bytes 2097152
  74.8 0.0 copy-done.2
  74.9 0.7 copy.19
  75.5 0.0 copy-done.1
  75.5 0.0 copy-start.3
  75.5 0.8 %copy.20 = f32[1024,128]{1,0:T(8,128)} copy(f32[1024,128]{1,0:T(8,128)S(1)} %bitcast.13) | data formatting | bytes 1048576
  76.3 0.0 copy-done.3
  76.3 0.5 copy.21
Async XLA Ops:
  71.8 2.1 %copy-start = (f32[2048,128]{1,0:T(8,128)S(1)}, f32[2048,128]{1,0:T(8,128)}, u32[]{:S(2)}) copy-start(f32[2048,128]{1,0:T(8,128)} %get-tuple-element.10) | copy-start | bytes 3145732
  73.9 1.0 %copy-start.2 = (f32[64,512]{1,0:T(8,128)S(1)}, f32[64,512]{1,0:T(8,128)}, u32[]{:S(2)}) copy-start(f32[64,512]{1,0:T(8,128)} %get-tuple-element.21) | copy-start | bytes 393220
  73.9 1.7 %copy-start.1 = (f32[32,32,128]{2,1,0:T(8,128)S(1)}, f32[32,32,128]{2,1,0:T(8,128)}, u32[]{:S(2)}) copy-start(f32[32,32,128]{2,1,0:T(8,128)} %get-tuple-element.13) | copy-start | bytes 1572868
  75.5 0.8 %copy-start.3 = (f32[1,128]{1,0:T(1,128)S(1)}, f32[1,128]{1,0:T(1,128)}, u32[]{:S(2)}) copy-start(f32[1,128]{1,0:T(1,128)} %get-tuple-element.14) | copy-start | bytes 1540

commit v4 on v3

--- a/solution.py
+++ b/solution.py
@@ -120,14 +120,14 @@
     lax.fori_loop(0, bh.shape[1] // width, one, 0)
 
 
-def make_grad_weight(oh, ol, pgh, pgl, acc, column_sums, scale, half):
+def make_grad_weight(oh, ol, pgh, pgl, acc, column_sums, scale, quarter, count=1):
     slots, held, _ = acc.shape
     piece = held - 8
-    group = 256 // piece
+    group = min(256 // piece, slots // 4)
     step = group * piece
 
     def one(turn, carry):
-        k = half * (slots // group // 2) + turn
+        k = quarter * (slots // group // 4) + turn
         rows = pl.ds(pl.multiple_of(k * step, step), step)
         ph = pgh[...]
         r = mm(oh[rows, :], jnp.concatenate([ph, pgl[...]], axis=1), NN)
@@ -137,7 +137,7 @@
             acc[k * group + g, piece:, :] = column_sums * scale
         return carry
 
-    lax.fori_loop(0, slots // group // 2, one, 0)
+    lax.fori_loop(0, slots // group // 4 * count, one, 0)
 
 
 def make_pair_out(oh, ol, w, bias, out, width, first, last):
@@ -237,6 +237,17 @@
 
         lax.fori_loop(0, 1 << q, one, 0)
 
+    def add_weight(quarter):
+        size = 1 << (levels - 2)
+        start = quarter * size
+        came = (1 << (levels - 1)) + (quarter % 2) * size
+
+        def one(k, carry):
+            w_acc[start + k] = w_acc[start + k] + w_in[came + k]
+            return carry
+
+        lax.fori_loop(0, size, one, 0)
+
     def next_right(t):
         return (
             gather(b_one, slot, t, partner[steps_one[t]]),
@@ -264,7 +275,7 @@
         w[e * C : (e + 1) * C, :] = w_cube[:, e, :]
     column_sums = split_grad(pg, pgh, pgl)
     groups = pgh.shape[0] // (2 * tj)
-    cuts = [groups // 8 + k * (groups - groups // 8) // (bits - 2) for k in range(bits - 1)]
+    cuts = [min(groups, groups // 8 + k * 5 * groups // 8) for k in range(bits - 2)] + [groups]
     make_grad_outer(pgh, pgl, w, gh, gl, tj, 0, cuts[0])
     for t in range(1, bits - 1):
         await_right(right_copy)
@@ -279,32 +290,36 @@
     r_copy.wait()
     add(r_acc, r_in, slot, bits - 1)
     r_copy = next_scatter(1)
-    await_right(right_copy)
-
+    right_copy[0].wait()
     split_right(b_one, steps_one, bh, bl, 0, 4 * tj)
+    right_copy[1].wait()
     split_right(b_two, steps_two, bh, bl, half_cols, 4 * tj)
     make_outer(a, bh, bl, oh, ol, tj)
     r_copy.wait()
     add(r_acc, r_in, slot, bits - 2)
     r_copy = next_scatter(2)
-    make_grad_weight(oh, ol, pgh, pgl, w_acc, column_sums, scale, 1 - order_bit[0])
+    weight = functools.partial(make_grad_weight, oh, ol, pgh, pgl, w_acc, column_sums, scale)
+    mine_first, mine_last = 2 * order_bit[0] + 1 - order_bit[1], 2 * order_bit[0] + order_bit[1]
+    weight(2 - 2 * order_bit[0], 2)
     w_copy = next_weight(0)
-    make_grad_weight(oh, ol, pgh, pgl, w_acc, column_sums, scale, order_bit[0])
+    weight(mine_first)
     w_copy.wait()
-    add(w_acc, w_in, w_slot, levels - 1)
+    add_weight(mine_first)
     w_copy = next_weight(1)
+    weight(mine_last)
+    add_weight(mine_last)
     for u in range(3, bits):
         r_copy.wait()
         add(r_acc, r_in, slot, bits - u)
         r_copy = next_scatter(u)
     size = gh.shape[0] // 2
     make_grad_left(bh, bl, gh, gl, l_part, 0, size)
-    make_grad_left(bh, bl, gh, gl, l_part, size, 2 * size)
-    left_copy = send(l_part.at[1 - col], l_in, across)
     w_copy.wait()
     add(w_acc, w_in, w_slot, levels - 2)
     exchanged = [send(w_acc.at[to], w_in.at[d], device) for d, device, to in others]
-    at = [groups * k // 8 for k in (0, 3, 5, 8)]
+    make_grad_left(bh, bl, gh, gl, l_part, size, 2 * size)
+    left_copy = send(l_part.at[1 - col], l_in, across)
+    at = [groups * k // 8 for k in (0, 1, 4, 7, 8)]
     make_pair_out(oh, ol, w, bias, out, 2 * tj, at[0], at[1])
     for copy in exchanged:
         copy.wait()
@@ -323,6 +338,7 @@
     make_pair_out(oh, ol, w, bias, out, 2 * tj, at[2], at[3])
     w_copy.wait()
     w_copy = gather(w_all, w_slot, levels - 1, order[0])
+    make_pair_out(oh, ol, w, bias, out, 2 * tj, at[3], at[4])
     r_copy.wait()
     add(r_acc, r_in, slot, 0)
     grad_right[...] = r_acc[slot]

time: 77 us -> 76.1 us (0.988)
  Pallas kernels: 69.2 us -> 68.3 us
    pallas_call x1, Pallas kernels: 69.2 us -> 68.3 us  [fast(): pl.pallas_call(functools.partial(kernel, n, tj, 1.0 / (ti * n)), out_shap...]
where the time goes in v4:
time: 76.1 us; the launch traced here: 75.9 us
  Pallas kernels  68.3 us (90%)
  local copies, waits for them, and re-layouts  6.95 us (9%)
    pallas_call x1, Pallas kernels, fast(): pl.pallas_call(functools.partial(kernel, n, tj, 1.0 / (ti * n)), out_shap...  68.3 us
    unnamed x12, local copies, waits for them, and re-layouts  2.97 us
    reshape x2, local copies, waits for them, and re-layouts, fast(): grad_right.reshape(-1, C, tj).transpose(0, 2, 1).reshape(right.shape)  2.08 us

profile of v4, /device:TPU:0, one launch (start us, length us, event | category | flops | bytes accessed | tf_op | source)
XLA Modules:
  0.0 75.9 jit_solution(931083983265658838)
XLA Ops:
  0.6 1.1 %reshape.40 = f32[8,128,32]{2,1,0:T(8,128)S(1)} reshape(f32[8,4096]{1,0:T(8,128)} %param.6) | data formatting | bytes 262144 | tf_op jit(solution)/shard_map/reshape | solution.py:364
  1.7 0.8 %copy.12 = f32[8,32,128]{2,0,1:T(8,128)} copy(f32[8,32,128]{1,2,0:T(8,128)S(1)} %bitcast.11) | data formatting | bytes 262144 | tf_op jit(solution)/shard_map/transpose | solution.py:364
  2.5 68.3 %outer_product_mean.1 = (f32[2048,128]{1,0:T(8,128)}, f32[64,512]{1,0:T(8,128)}, f32[8,4096]{1,0:T(8,128)}, f32[32,32,128]{2,1,0:T(8,128)}, f32[1,128]{1,0:T(1,128)}) custom-call(f32[64,512]{1,0:T(8,128)} %left.1, f32[8,4096]{1,0:T(8,128)} %bitcast.14, f32[2048,128]{1,0:T(8,128)} %bitcast.16, f32[32,32,128]{2,1,0:T(8,128)} %bitcast.17, f32[1,128]{1,0:T(1,128)} %bitcast.18), custom_call_target="tpu_custom_call" | custom-call | flops 9663676416 | bytes 8388608 | tf_op jit(solution)/shard_map/outer_product_mean/pallas_call | solution.py:387
  70.8 0.0 copy-start
  70.8 1.2 %copy.13 = f32[8,32,128]{1,2,0:T(8,128)S(1)} copy(f32[8,32,128]{2,0,1:T(8,128)} %bitcast.15) | data formatting | bytes 262144 | tf_op jit(solution)/shard_map/reshape | solution.py:409
  72.0 0.9 %reshape.47 = f32[8,4096]{1,0:T(8,128)} reshape(f32[8,128,32]{2,1,0:T(8,128)S(1)} %bitcast.10) | data formatting | bytes 262144 | tf_op jit(solution)/shard_map/reshape | solution.py:409
  72.9 0.0 copy-done
  72.9 0.0 copy-start.2
  72.9 0.0 copy-start.1
  72.9 1.0 %copy.18 = f32[16,128,128]{2,1,0:T(8,128)} copy(f32[16,128,128]{2,1,0:T(8,128)S(1)} %bitcast.12) | data formatting | bytes 2097152
  73.9 0.0 copy-done.2
  73.9 0.7 copy.19
  74.6 0.0 copy-done.1
  74.6 0.0 copy-start.3
  74.6 0.8 %copy.20 = f32[1024,128]{1,0:T(8,128)} copy(f32[1024,128]{1,0:T(8,128)S(1)} %bitcast.13) | data formatting | bytes 1048576
  75.4 0.0 copy-done.3
  75.4 0.5 copy.21
Async XLA Ops:
  70.8 2.1 %copy-start = (f32[2048,128]{1,0:T(8,128)S(1)}, f32[2048,128]{1,0:T(8,128)}, u32[]{:S(2)}) copy-start(f32[2048,128]{1,0:T(8,128)} %get-tuple-element.10) | copy-start | bytes 3145732
  72.9 1.0 %copy-start.2 = (f32[64,512]{1,0:T(8,128)S(1)}, f32[64,512]{1,0:T(8,128)}, u32[]{:S(2)}) copy-start(f32[64,512]{1,0:T(8,128)} %get-tuple-element.21) | copy-start | bytes 393220
  72.9 1.7 %copy-start.1 = (f32[32,32,128]{2,1,0:T(8,128)S(1)}, f32[32,32,128]{2,1,0:T(8,128)}, u32[]{:S(2)}) copy-start(f32[32,32,128]{2,1,0:T(8,128)} %get-tuple-element.13) | copy-start | bytes 1572868
  74.6 0.8 %copy-start.3 = (f32[1,128]{1,0:T(1,128)S(1)}, f32[1,128]{1,0:T(1,128)}, u32[]{:S(2)}) copy-start(f32[1,128]{1,0:T(1,128)} %get-tuple-element.14) | copy-start | bytes 1540
